TPU v7x, 512 devices: a whole 4x4x16 slice. The times are simulated.
512 devices in a mesh: tensor: 16 (over z), adapter: 32 (over y, x, core).
Axes of the slice: x: 4, y: 4, z: 16, core: 2. Of those that a mesh axis runs over, the one named last changes fastest.
Arguments:
- tokens: bfloat16 [8192, 8192], P('adapter', 'tensor'), may hold values from -6 to 6
- token_adapter_index: int32 [8192, 1], P('adapter'), may hold values from 0 to 127; in each aligned block of 256 rows (0 to 255, 256 to 511, ...) at most 8 rows name the same one
- adapter_table_row: int32 [128], replicated, may hold values from 0 to 127, each once
- key_value_weight: bfloat16 [8192, 2048], P('tensor'), may hold values from -0.09375 to 0.09375
- adapter_down_weight: bfloat16 [128, 8192, 128], P('adapter', 'tensor'), may hold values from -0.0625 to 0.0625
- adapter_up_weight: bfloat16 [128, 64, 2048], P('adapter'), may hold values from -0.75 to 0.75
Outputs:
- keys_values: bfloat16 [8192, 2048], P('adapter', 'tensor')
Inputs may be any that keep to these rules, and one draw needn't show every extreme that they name: `token_adapter_index`: among the 256 rows of one aligned block (one device along adapter), no adapter is named more than 8 times, a bound that some block reaches. `adapter_table_row`: each value once.
All inputs are finite; a program needn't handle non-finite values.
Results may differ from a plain program's by a relative error of at most 0.0035.
Values may be sent and summed in bfloat16 or wider, within the bound.
A program may use at most 64 MiB of HBM per device.

v0:
```python
import jax
import jax.numpy as jnp
from jax import lax
from jax.sharding import PartitionSpec as P

adapter_scale = 0.5


def per_device(
    tokens,
    token_adapter_index,
    adapter_table_row,
    key_value_weight,
    adapter_down_weight,
    adapter_up_weight,
):
    tok_rows, feature = tokens.shape
    columns = key_value_weight.shape[1]
    column_portion = columns // lax.axis_size("tensor")
    kv_width = columns // 2
    kept_count = adapter_down_weight.shape[0]
    rank_extent = adapter_down_weight.shape[2] // 2
    adapters_all = kept_count * lax.axis_size("adapter")
    slot_cap = max(2, max(tok_rows // 32, (tok_rows + adapters_all - 1) // adapters_all))
    frozen_columns = lax.psum_scatter(
        lax.dot_general(
            key_value_weight, tokens, (((0,), (1,)), ((), ())), preferred_element_type=jnp.float32
        ),
        "tensor",
        scatter_dimension=0,
        tiled=True,
    )
    token_ids = token_adapter_index[:, 0]
    table_iota = jnp.arange(adapters_all, dtype=jnp.int32)
    id_match = token_ids[:, None] == table_iota[None, :]
    table_pos = jnp.sum(jnp.where(id_match, adapter_table_row[None, :], 0), axis=1)
    hit_table = (table_pos[:, None] == table_iota[None, :]).astype(jnp.int32)
    running = jnp.cumsum(hit_table, axis=0) - 1
    within = jnp.sum(running * hit_table, axis=1)
    position_index = table_pos * slot_cap + within
    outgoing = (
        jnp.zeros((adapters_all * slot_cap, feature), tokens.dtype).at[position_index].set(tokens)
    )
    outgoing = outgoing.reshape(adapters_all, slot_cap, feature)
    received_rows = lax.all_to_all(outgoing, "adapter", split_axis=0, concat_axis=1, tiled=True)
    partial_rank = jnp.einsum(
        "plx,pxq->plq", received_rows, adapter_down_weight, preferred_element_type=jnp.float32
    )
    low_rank = lax.psum(partial_rank, "tensor").astype(jnp.bfloat16)
    column_offset = lax.axis_index("tensor") * column_portion
    upward_columns = lax.dynamic_slice_in_dim(adapter_up_weight, column_offset, column_portion, 2)
    rank_half = jnp.where(
        column_offset >= kv_width, low_rank[:, :, rank_extent:], low_rank[:, :, :rank_extent]
    )
    delta_cols = jnp.einsum(
        "esr,erc->esc", rank_half, upward_columns, preferred_element_type=jnp.float32
    )
    returned = lax.all_to_all(
        delta_cols.astype(jnp.bfloat16), "adapter", split_axis=1, concat_axis=0, tiled=True
    )
    flattened = returned.reshape(adapters_all * slot_cap, column_portion)
    update_rows = flattened[position_index]
    projected_output = frozen_columns.T + adapter_scale * update_rows.astype(jnp.float32)
    return projected_output.astype(jnp.bfloat16)


def solution(mesh):
    return jax.shard_map(
        per_device,
        mesh=mesh,
        in_specs=(
            P("adapter", "tensor"),
            P("adapter", None),
            P(),
            P("tensor", None),
            P("adapter", "tensor", None),
            P("adapter", None, None),
        ),
        out_specs=P("adapter", "tensor"),
        check_vma=False,
    )
```

profile of v0, /device:TPU:1, one launch (start us, length us, event | category | flops | bytes accessed | tf_op | source)
XLA Modules:
  0.0 139.6 jit_solution(10038024063526136345)
XLA Ops:
  6.5 0.0 copy-start
  6.5 0.0 reduce-scatter.2.cloned.1.call-start
  6.5 1.6 %copy-done = bf16[512,2048]{1,0:T(8,128)(2,1)S(1)} copy-done((bf16[512,2048]{1,0:T(8,128)(2,1)S(1)}, bf16[512,2048]{1,0:T(8,128)(2,1)}, u32[]{:S(2)}) %copy-start) | copy-done | bytes 2097176
  8.1 3.1 %fusion.14 = f32[2048,256]{1,0:T(8,128)} fusion(bf16[512,2048]{1,0:T(8,128)(2,1)S(1)} %copy-done, bf16[256,512]{1,0:T(8,128)(2,1)} %param.6), kind=kOutput, calls=%fused_computation.29 | convolution fusion | flops 536870912 | bytes 4456448 | tf_op jit(solution)/shard_map/dot_general | solution.py:26
  11.2 0.0 copy-start.1
  11.2 0.0 copy-start.2
  11.2 0.0 reduce-scatter.2.cloned.1.call-update
  11.2 0.7 copy-done.1
  11.9 0.0 copy-done.2
  11.9 0.2 select_reduce_fusion
  12.0 0.1 copy.18
  12.2 0.2 fusion.7
  12.4 0.1 add_add_fusion
  12.5 0.2 fusion.8
  12.7 3.0 %scatter_custom_fusion = bf16[1024,512]{1,0:T(8,128)(2,1)} fusion(s32[256]{0:T(256)S(1)} %bitcast.34, bf16[256,512]{1,0:T(8,128)(2,1)} %param.6, bf16[]{:T(256)} %constant.7.clone.1), kind=kCustom, calls=%fused_computation.6 | custom fusion | bytes 1049088 | tf_op jit(solution)/shard_map/scatter | solution.py:42
  15.8 10.5 %all-to-all-start = ((bf16[128,8,512]{2,1,0:T(8,128)(2,1)}), bf16[128,8,512]{2,1,0:T(8,128)(2,1)S(1)}, u32[]{:S(2)}, u32[]{:S(2)}) async-start(bf16[128,8,512]{2,1,0:T(8,128)(2,1)} %bitcast.8), calls=%async_computation.1 | async-start | bytes 2097152 | tf_op jit(solution)/shard_map/all_to_all | solution.py:45
  26.2 17.3 %all-to-all-done = bf16[128,8,512]{2,1,0:T(8,128)(2,1)S(1)} async-done(((bf16[128,8,512]{2,1,0:T(8,128)(2,1)}), bf16[128,8,512]{2,1,0:T(8,128)(2,1)S(1)}, u32[]{:S(2)}, u32[]{:S(2)}) %all-to-all-start) | async-done | bytes 1048608 | tf_op jit(solution)/shard_map/all_to_all | solution.py:45
  43.5 2.3 %fusion = f32[4,256,128]{2,1,0:T(8,128)} fusion(bf16[4,512,128]{2,1,0:T(8,128)(2,1)} %param.10, bf16[4,32,8,512]{3,2,0,1:T(8,128)(2,1)S(1)} %bitcast.31), kind=kOutput, calls=%fused_computation.3 | convolution fusion | flops 134217728 | bytes 2097152 | tf_op jit(solution)/shard_map/plx,pxq->plq/dot_general | solution.py:46
  45.8 59.1 %all-reduce.1 = bf16[4,256,128]{2,1,0:T(8,128)(2,1)S(1)} all-reduce(f32[4,256,128]{2,1,0:T(8,128)} %fusion), channel_id=1, replica_groups=mesh['tensor'=16,'adapter'=32] {'tensor'}, use_global_device_ids=true, to_apply=%region_6.7 | all-reduce | flops 131072 | bytes 786432 | tf_op jit(solution)/shard_map/psum | solution.py:49
  104.9 1.1 convolution_convert_fusion
  106.0 0.9 copy.22
  107.0 14.1 %all-to-all-start.1 = ((bf16[4,256,128]{2,0,1:T(4,128)(2,1)}), bf16[4,256,128]{2,0,1:T(4,128)(2,1)S(1)}, u32[]{:S(2)}, u32[]{:S(2)}) async-start(bf16[4,256,128]{2,0,1:T(4,128)(2,1)} %copy.22), calls=%async_computation.2 | async-start | bytes 524288 | tf_op jit(solution)/shard_map/all_to_all | solution.py:58
  121.1 8.9 %all-to-all-done.1 = bf16[4,256,128]{2,0,1:T(4,128)(2,1)S(1)} async-done(((bf16[4,256,128]{2,0,1:T(4,128)(2,1)}), bf16[4,256,128]{2,0,1:T(4,128)(2,1)S(1)}, u32[]{:S(2)}, u32[]{:S(2)}) %all-to-all-start.1) | async-done | bytes 262176 | tf_op jit(solution)/shard_map/all_to_all | solution.py:58
  130.1 0.9 gather_fusion
  130.9 0.1 copy.24
  131.0 0.0 reduce-scatter.2.cloned.1.call-done
  131.1 0.9 fusion.9
  132.0 0.7 copy.25
  (8 shorter events, 0.1 us)
Async XLA Ops:
  6.5 1.6 %copy-start = (bf16[512,2048]{1,0:T(8,128)(2,1)S(1)}, bf16[512,2048]{1,0:T(8,128)(2,1)}, u32[]{:S(2)}) copy-start(bf16[512,2048]{1,0:T(8,128)(2,1)} %param.9) | copy-start | bytes 6291460
  6.5 124.5 %reduce-scatter.2.cloned.1.call-start = ((), (), s32[]{:S(2)}) async-start(), calls=%async_computation.3 | async-start | bytes 2228224 | tf_op jit(solution)/shard_map/reduce_scatter | solution.py:25
  11.2 0.7 copy-start.1
  11.2 0.7 copy-start.2
  15.8 27.8 %all-to-all-start = ((bf16[128,8,512]{2,1,0:T(8,128)(2,1)}), bf16[128,8,512]{2,1,0:T(8,128)(2,1)S(1)}, u32[]{:S(2)}, u32[]{:S(2)}) async-start(bf16[128,8,512]{2,1,0:T(8,128)(2,1)} %bitcast.8), calls=%async_computation.1 | async-start | bytes 2097152 | tf_op jit(solution)/shard_map/all_to_all | solution.py:45
  107.0 23.0 %all-to-all-start.1 = ((bf16[4,256,128]{2,0,1:T(4,128)(2,1)}), bf16[4,256,128]{2,0,1:T(4,128)(2,1)S(1)}, u32[]{:S(2)}, u32[]{:S(2)}) async-start(bf16[4,256,128]{2,0,1:T(4,128)(2,1)} %copy.22), calls=%async_computation.2 | async-start | bytes 524288 | tf_op jit(solution)/shard_map/all_to_all | solution.py:58
Sparse Core Ops, SparseCore 0:
  11.3 70.4 reduce-scatter.1
where the time goes:
time: 140 us
  blocking collectives  59.1 us (42%)
  waiting for transfers between devices  26.2 us (19%)
  starting transfers between devices  24.6 us (18%)
  between operations  13.5 us (10%)
  local copies, waits for them, and re-layouts  8.08 us (6%)
  matrix products  6.46 us (5%)
  other arithmetic  1.6 us (1%)
    psum x1, blocking collectives, per_device(): low_rank = lax.psum(partial_rank, 'tensor').astype(jnp.bfloat16)  59.1 us
    all_to_all x1, waiting for transfers between devices, per_device(): lax.all_to_all(outgoing, 'adapter', split_axis=0, concat_axis=1, tiled=True)  17.3 us
    all_to_all x1, starting transfers between devices, per_device(): lax.all_to_all(delta_cols.astype(jnp.bfloat16), 'adapter', split_axis=1,...  14.1 us
    all_to_all x1, starting transfers between devices, per_device(): lax.all_to_all(outgoing, 'adapter', split_axis=0, concat_axis=1, tiled=True)  10.5 us
    all_to_all x1, waiting for transfers between devices, per_device(): lax.all_to_all(delta_cols.astype(jnp.bfloat16), 'adapter', split_axis=1,...  8.89 us
    dot_general x1, matrix products, per_device(): lax.dot_general(key_value_weight, tokens, (((0,), (1,)), ((), ())), prefe...  3.06 us
    scatter x1, local copies, waits for them, and re-layouts, per_device(): jnp.zeros((adapters_all * slot_cap, feature), tokens.dtype)  3.03 us
  transfers between devices with their start and end apart: 3, of which 2 were waited for; matrix products, arithmetic and copies ran while one was open for 7% of the time, Pallas kernels for 0%

commit v1 on v0

v1 whole, which is shorter than its diff:
```python
import jax
import jax.numpy as jnp
from jax import lax
from jax.experimental import pallas as pl
from jax.experimental.pallas import tpu as pltpu
from jax.sharding import PartitionSpec as P

adapter_scale = 0.5
MESH = pl.DeviceIdType.MESH
F32, BF16, I32 = jnp.float32, jnp.bfloat16, jnp.int32

NY, NX, NC, NZ = 4, 4, 2, 16
NA = NY * NX * NC
TOK, FEAT, COLS = 256, 512, 128
HELD, CAP, RANK2 = 4, 8, 128
MSG = HELD * CAP
GROUP = NX * NC
ROWS = GROUP * MSG
GROUPS = (2, 1, 3, 0)
OFFSETS = ((2, 0), (2, 1), (1, 0), (1, 1), (3, 0), (3, 1), (0, 1), (0, 0))


def iota(shape, dim):
    return lax.broadcasted_iota(I32, shape, dim)


def dot(a, b):
    return jnp.dot(a, b, preferred_element_type=F32)


def kernel(
    ids_ref, table_ref, tokens_hbm, kv_hbm, down_hbm, up_hbm, out_ref,
    tok, kv, down, up, sbuf, rbuf, lbuf, ret, place, zsend, zrecv, pack,
    b1, own, r1, w2, r2,
    load_sem, self_sem, tok_send, tok_recv, ret_send, ret_recv, zs_send, zs_recv, zg_send, zg_recv,
    l1_send, l1_recv, l2_send, l2_recv, up_send, up_recv,
):
    a, z = lax.axis_index("adapter"), lax.axis_index("tensor")
    y, x, c = lax.div(a, GROUP), lax.rem(lax.div(a, NC), NX), lax.rem(a, NC)

    def at(dy, dx, dc):
        return (
            lax.rem(y + dy + NY, NY) * GROUP + lax.rem(x + dx + NX, NX) * NC + lax.rem(c + dc + NC, NC)
        )

    def along_z(dz):
        return lax.rem(z + dz + NZ, NZ)

    def plane_copy(src, dst, send, recv, peer):
        return pltpu.make_async_remote_copy(
            src, dst, send, recv, device_id={"adapter": peer}, device_id_type=MESH
        )

    def z_copy(src, dst, send, recv, peer):
        return pltpu.make_async_remote_copy(
            src, dst, send, recv, device_id={"tensor": peer}, device_id_type=MESH
        )

    def wait_bytes(ref, sem):
        pltpu.make_async_copy(ref, ref, sem).wait()

    loads = [
        pltpu.make_async_copy(tokens_hbm, tok, load_sem.at[0]),
        pltpu.make_async_copy(kv_hbm, kv, load_sem.at[1]),
        pltpu.make_async_copy(down_hbm, down, load_sem.at[2]),
        pltpu.make_async_copy(
            up_hbm.at[:, :, pl.ds(pl.multiple_of(z * COLS, COLS), COLS)], up.at[y, x, c], load_sem.at[3]
        ),
    ]
    for load in loads:
        load.start()

    barrier = pltpu.get_barrier_semaphore()

    @pl.loop(1, NA)
    def _(k):
        pl.semaphore_signal(barrier, 1, device_id={"adapter": lax.rem(a + k, NA)}, device_id_type=MESH)

    @pl.loop(1, NZ)
    def _(k):
        pl.semaphore_signal(barrier, 1, device_id={"tensor": lax.rem(z + k, NZ)}, device_id_type=MESH)

    names = iota((128, TOK), 0)
    table = jnp.broadcast_to(table_ref[...].astype(F32), (8, 128)).astype(BF16)
    hit_id = (names == ids_ref[...]).astype(F32).astype(BF16)
    row = dot(table, hit_id)[0:1]
    hit = names == row.astype(I32)
    hit_f = hit.astype(F32)
    square0, square1 = iota((TOK, TOK), 0), iota((TOK, TOK), 1)
    earlier = dot(hit_f.astype(BF16), (square0 < square1).astype(F32).astype(BF16))
    within = jnp.sum(hit_f * earlier, axis=0, keepdims=True)
    slot = row.astype(I32) * CAP + within.astype(I32)

    def slots_of(r):
        return (
            lax.rem(x + lax.div(r, 2 * MSG), NX) * (NC * MSG)
            + lax.rem(c + lax.div(r, MSG), NC) * MSG
            + lax.rem(r, MSG)
        )

    loads[0].wait()
    in_row = slots_of(square0)
    token_copies = {}
    for turn, dy in enumerate(GROUPS):
        first = lax.rem(y + dy, NY) * ROWS
        chosen = (in_row == slot - first).astype(F32).astype(BF16)
        sbuf[dy * GROUP : (dy + 1) * GROUP] = dot(chosen, tok[...]).astype(BF16).reshape(GROUP, MSG, FEAT)
        if turn == 0:
            pl.semaphore_wait(barrier, NA - 1 + NZ - 1)
        for dx, dc in OFFSETS:
            k = dy * GROUP + dx * NC + dc
            if k == 0:
                token_copies[k] = pltpu.make_async_copy(sbuf.at[0], rbuf.at[0], self_sem)
            else:
                token_copies[k] = plane_copy(sbuf.at[k], rbuf.at[k], tok_send, tok_recv.at[dy], at(dy, dx, dc))
            token_copies[k].start()

    loads[1].wait()

    def part(dz, j):
        d = along_z(dz + 4 * j)
        return dot(tok[...], kv[:, pl.ds(pl.multiple_of(d * COLS, COLS), COLS)])

    half = TOK // 2
    for j in (2, 1, 3, 0):
        b1[0, j] = part(1, j).astype(BF16)
        z_copy(b1.at[0, j], r1.at[0, j], l1_send, l1_recv.at[j], along_z(1)).start()
        b1[1, j] = part(-1, j).astype(BF16)
        z_copy(b1.at[1, j], r1.at[1, j], l1_send, l1_recv.at[j], along_z(-1)).start()
        b1[2, j] = part(2, j).astype(BF16)
        i = (j + 1) % 4
        low, high = pl.ds(0, half), pl.ds(half, half)
        z_copy(b1.at[2, j, high], r1.at[2, j, high], l1_send, l1_recv.at[j], along_z(2)).start()
        z_copy(b1.at[2, j, low], r1.at[2, i, low], l1_send, l1_recv.at[i], along_z(-2)).start()

    loads[3].wait()

    def first_axis(k):
        return jnp.where(c == 0, at(0, k, 0), at(k, 0, 0))

    def second_axis(k):
        return jnp.where(c == 0, at(k, 0, 0), at(0, k, 0))

    for k in (2, 1, 3):
        plane_copy(up.at[y, x, c], up.at[y, x, c], up_send.at[0], up_recv.at[0], first_axis(k)).start()

    for j in range(4):
        own[j] = part(0, j)

    diagonal = square0 == square1
    ones = jnp.ones((TOK, 128), BF16)
    row_at = dot(jnp.where(diagonal, row, 0.0).astype(BF16), ones)
    within_at = dot(jnp.where(diagonal, within, 0.0).astype(BF16), ones)
    slot_at = (row_at * CAP + within_at).astype(I32)
    slot_at = jnp.concatenate([slot_at, slot_at], axis=1)
    in_row = slots_of(square1)
    for dy in range(NY):
        first = lax.rem(y + dy, NY) * ROWS
        place[dy] = (in_row == slot_at - first).astype(F32).astype(BF16)

    loads[2].wait()
    left = jnp.concatenate([down[0], down[1]], axis=1)
    right = jnp.concatenate([down[2], down[3]], axis=1)
    which = lax.rem(lax.div(iota((ROWS, RANK2), 0), CAP), HELD)
    for turn, j in enumerate((2, 1, 3, 0)):
        wait_bytes(r1.at[:, j], l1_recv.at[j])
        window = own[j] + r1[0, j].astype(F32) + r1[1, j].astype(F32) + r1[2, j].astype(F32)
        if j == 0:
            own[0] = window
        else:
            w2[j - 1] = window.astype(BF16)
            z_copy(w2.at[j - 1], r2.at[j - 1], l2_send, l2_recv, along_z(4 * j)).start()

        dy = GROUPS[turn]
        lo = dy * GROUP
        if dy == 0:
            wait_bytes(rbuf.at[1:GROUP], tok_recv.at[0])
            token_copies[0].wait()
        else:
            wait_bytes(rbuf.at[lo : lo + GROUP], tok_recv.at[dy])
        arrived = rbuf[lo : lo + GROUP].reshape(ROWS, FEAT)
        l01, l23 = dot(arrived, left), dot(arrived, right)
        low_rank = jnp.where(
            which < 2,
            jnp.where(which == 0, l01[:, :RANK2], l01[:, RANK2:]),
            jnp.where(which == 2, l23[:, :RANK2], l23[:, RANK2:]),
        ).astype(BF16)
        lbuf[lo : lo + GROUP] = low_rank.reshape(GROUP, MSG, RANK2)
        for dx, dc in OFFSETS:
            k = lo + dx * NC + dc
            if k == 0:
                ret[0] = lbuf[0]
            else:
                plane_copy(lbuf.at[k], ret.at[k], ret_send, ret_recv.at[dy], at(-dy, -dx, -dc)).start()

    wait_bytes(up.at[0, 0:3, 0], up_recv.at[0])

    @pl.when(c == 0)
    def _():
        for k in (2, 1, 3):
            plane_copy(up.at[y, :, 0], up.at[y, :, 0], up_send.at[1], up_recv.at[1], at(k, 0, 0)).start()

    @pl.when(c == 1)
    def _():
        for k in (2, 1, 3):
            plane_copy(up.at[:, x, 1], up.at[:, x, 1], up_send.at[1], up_recv.at[1], at(0, k, 0)).start()

    low_rank = jnp.zeros((TOK, RANK2), F32)
    for dy in GROUPS:
        lo = dy * GROUP
        wait_bytes(ret.at[max(lo, 1) : lo + GROUP], ret_recv.at[dy])
        low_rank += dot(place[dy], ret[lo : lo + GROUP].reshape(ROWS, RANK2))
    upper, lower = low_rank[:half], low_rank[half:]
    first_lanes = iota((half, RANK2), 1) < RANK2 // 2
    keys = jnp.where(first_lanes, upper, pltpu.roll(lower, RANK2 // 2, 1))
    values = jnp.where(first_lanes, pltpu.roll(upper, RANK2 // 2, 1), lower)
    zsend[0:8] = keys.astype(BF16).reshape(8, 16, RANK2)
    zsend[8:16] = values.astype(BF16).reshape(8, 16, RANK2)
    for k in (8, 7, 9, 6, 10, 5, 11, 4, 12, 3, 13, 2, 14, 1, 15):
        z_copy(zsend.at[along_z(k)], zrecv.at[k - 1], zs_send, zs_recv, along_z(k)).start()

    wait_bytes(r2, l2_recv)
    own[0] = own[0] + r2[0].astype(F32) + r2[1].astype(F32) + r2[2].astype(F32)

    wait_bytes(up.at[0:3, :, 0], up_recv.at[1])
    other = at(0, 0, 1)
    plane_copy(up.at[:, :, c], up.at[:, :, c], up_send.at[2], up_recv.at[2], other).start()

    wait_bytes(zrecv, zs_recv)
    total = zsend[z].astype(F32)
    for k in range(NZ - 1):
        total += zrecv[k].astype(F32)
    spot, side = lax.rem(z, 8), lax.div(z, 8) * 8
    pack[spot] = total.astype(BF16)
    for k in (4, 3, 5, 2, 6, 1, 7):
        z_copy(pack.at[spot], pack.at[spot], zg_send, zg_recv, side + lax.rem(spot + k, 8)).start()

    wait_bytes(up.at[:, :, 0], up_recv.at[2])
    wait_bytes(pack.at[0:7], zg_recv)

    full = pack[...].reshape(half, RANK2).astype(F32)
    turned = pltpu.roll(full, RANK2 // 2, 1)
    twice = jnp.concatenate(
        [jnp.where(first_lanes, full, turned), jnp.where(first_lanes, turned, full)], axis=0
    ).astype(BF16)
    twice = jnp.concatenate([twice, twice], axis=1)
    lane = lax.div(iota((TOK, 256), 1), RANK2 // 2)
    shifted = jnp.concatenate([row_at, row_at], axis=1).astype(I32) - lane
    delta = jnp.zeros((TOK, COLS), F32)
    for h in range(NA):
        block = jnp.where(shifted == HELD * h, twice, jnp.zeros_like(twice))
        delta += dot(block, up[h // GROUP, h // NC % NX, h % NC].reshape(HELD * 64, COLS))
    result = own[0] + adapter_scale * delta.astype(BF16).astype(F32)
    out_ref[...] = result.astype(BF16)

    wait_bytes(sbuf.at[1:NA], tok_send)
    wait_bytes(lbuf.at[1:NA], ret_send)
    wait_bytes(b1, l1_send)
    wait_bytes(w2, l2_send)
    wait_bytes(zrecv, zs_send)
    wait_bytes(pack.at[0:7], zg_send)
    wait_bytes(up.at[0, 0:3, 0], up_send.at[0])
    wait_bytes(up.at[0:3, :, 0], up_send.at[1])
    wait_bytes(up.at[:, :, 0], up_send.at[2])


def per_device(tokens, token_adapter_index, adapter_table_row, kv_weight, down_weight, up_weight):
    dma = pltpu.SemaphoreType.DMA
    vmem = pltpu.VMEM
    call = pl.pallas_call(
        kernel,
        out_shape=jax.ShapeDtypeStruct((TOK, COLS), BF16),
        in_specs=[pl.BlockSpec(memory_space=pltpu.VMEM)] * 2 + [pl.BlockSpec(memory_space=pl.ANY)] * 4,
        out_specs=pl.BlockSpec(memory_space=pltpu.VMEM),
        scratch_shapes=[
            vmem((TOK, FEAT), BF16),
            vmem((FEAT, NZ * COLS), BF16),
            vmem((HELD, FEAT, RANK2), BF16),
            vmem((NY, NX, NC, HELD, RANK2 // 2, COLS), BF16),
            vmem((NA, MSG, FEAT), BF16),
            vmem((NA, MSG, FEAT), BF16),
            vmem((NA, MSG, RANK2), BF16),
            vmem((NA, MSG, RANK2), BF16),
            vmem((NY, TOK, ROWS), BF16),
            vmem((NZ, 16, RANK2), BF16),
            vmem((NZ - 1, 16, RANK2), BF16),
            vmem((8, 16, RANK2), BF16),
            vmem((3, 4, TOK, COLS), BF16),
            vmem((4, TOK, COLS), F32),
            vmem((3, 4, TOK, COLS), BF16),
            vmem((3, TOK, COLS), BF16),
            vmem((3, TOK, COLS), BF16),
            dma((4,)),
            dma,
            dma,
            dma((NY,)),
            dma,
            dma((NY,)),
            dma,
            dma,
            dma,
            dma,
            dma,
            dma((4,)),
            dma,
            dma,
            dma((3,)),
            dma((3,)),
        ],
        compiler_params=pltpu.CompilerParams(
            collective_id=0, has_side_effects=True, vmem_limit_bytes=40 << 20
        ),
        name="lora_kv",
    )
    return call(
        token_adapter_index.reshape(1, TOK),
        adapter_table_row.reshape(1, 128),
        tokens,
        kv_weight,
        down_weight,
        up_weight,
    )


def solution(mesh):
    return jax.shard_map(
        per_device,
        mesh=mesh,
        in_specs=(
            P("adapter", "tensor"),
            P("adapter", None),
            P(),
            P("tensor", None),
            P("adapter", "tensor", None),
            P("adapter", None, None),
        ),
        out_specs=P("adapter", "tensor"),
        check_vma=False,
    )
```

time: 140 us -> 64 us (0.46)
  blocking collectives: 59.1 us -> 0 us
  Pallas kernels: 0 us -> 56.6 us
  waiting for transfers between devices: 26.2 us -> 0 us
  starting transfers between devices: 24.6 us -> 0 us
  between operations: 13.5 us -> 0.02 us
  matrix products: 6.46 us -> 0 us
  other arithmetic: 1.6 us -> 0 us
    psum x1 -> x0, blocking collectives: 59.1 us -> none  [per_device(): low_rank = lax.psum(partial_rank, 'tensor').astype(jnp.bfloat16)]
    pallas_call x0 -> x1, Pallas kernels: none -> 56.6 us  [per_device(): call(token_adapter_index.reshape(1, TOK), adapter_table_row.reshape(1, 12...]
    all_to_all x2 -> x0, waiting for transfers between devices: 26.2 us -> none  [the longest x1 17.3 us: per_device(): lax.all_to_all(outgoing, 'adapter', split_axis=0, concat_axis=1, tiled=True)]
    all_to_all x2 -> x0, starting transfers between devices: 24.6 us -> none  [the longest x1 14.1 us: per_device(): lax.all_to_all(delta_cols.astype(jnp.bfloat16), 'adapter', split_axis=1,...]
    dot_general x3 -> x0, matrix products: 6.46 us -> none  [the longest x1 3.06 us: per_device(): lax.dot_general(key_value_weight, tokens, (((0,), (1,)), ((), ())), prefe...]
    unnamed x6 -> x13, local copies, waits for them, and re-layouts: 2.24 us -> 6.77 us
    scatter x1 -> x0, local copies, waits for them, and re-layouts: 3.03 us -> none  [per_device(): jnp.zeros((adapters_all * slot_cap, feature), tokens.dtype)]
    convert_element_type x2 -> x0, local copies, waits for them, and re-layouts: 1.67 us -> none  [the longest x1 0.93 us: per_device(): delta_cols.astype(jnp.bfloat16)]
  transfers between devices with their start and end apart: 3 -> 0, of which waited for: 2 -> 0; matrix products, arithmetic and copies ran while one was open for 7% -> 0% of each run, Pallas kernels for 0% -> 0%
where the time goes in v1:
time: 64 us; the launch traced here: 63.4 us
  Pallas kernels  56.6 us (88%)
  local copies, waits for them, and re-layouts  6.77 us (11%)
    pallas_call x1, Pallas kernels, per_device(): call(token_adapter_index.reshape(1, TOK), adapter_table_row.reshape(1, 12...  56.6 us
    unnamed x13, local copies, waits for them, and re-layouts  6.77 us

profile of v1, /device:TPU:1, one launch (start us, length us, event | category | flops | bytes accessed | tf_op | source)
XLA Modules:
  0.0 63.4 jit_solution(5360803216702584875)
XLA Ops:
  0.0 0.0 copy-start
  0.0 1.6 %copy-done = bf16[512,2048]{1,0:T(8,128)(2,1)S(1)} copy-done((bf16[512,2048]{1,0:T(8,128)(2,1)S(1)}, bf16[512,2048]{1,0:T(8,128)(2,1)}, u32[]{:S(2)}) %copy-start) | copy-done | bytes 2097176
  1.6 0.0 copy-start.1
  1.6 1.2 %copy-done.1 = bf16[4,64,2048]{2,1,0:T(8,128)(2,1)S(1)} copy-done((bf16[4,64,2048]{2,1,0:T(8,128)(2,1)S(1)}, bf16[4,64,2048]{2,1,0:T(8,128)(2,1)}, u32[]{:S(2)}) %copy-start.1) | copy-done | bytes 1048600
  2.8 0.0 copy-start.2
  2.8 1.0 %copy-done.2 = bf16[4,512,128]{2,1,0:T(8,128)(2,1)S(1)} copy-done((bf16[4,512,128]{2,1,0:T(8,128)(2,1)S(1)}, bf16[4,512,128]{2,1,0:T(8,128)(2,1)}, u32[]{:S(2)}) %copy-start.2) | copy-done | bytes 524312
  3.9 0.0 copy-start.3
  3.9 0.9 %copy-done.3 = bf16[256,512]{1,0:T(8,128)(2,1)S(1)} copy-done((bf16[256,512]{1,0:T(8,128)(2,1)S(1)}, bf16[256,512]{1,0:T(8,128)(2,1)}, u32[]{:S(2)}) %copy-start.3) | copy-done | bytes 262168
  4.8 0.0 copy-start.4
  4.8 0.7 %copy-done.4 = s32[256,1]{0,1:T(1,128)S(1)} copy-done((s32[256,1]{0,1:T(1,128)S(1)}, s32[256,1]{0,1:T(1,128)}, u32[]{:S(2)}) %copy-start.4) | copy-done | bytes 1048
  5.5 0.0 copy-start.5
  5.5 0.7 %copy-done.5 = s32[128]{0:T(128)S(1)} copy-done((s32[128]{0:T(128)S(1)}, s32[128]{0:T(128)}, u32[]{:S(2)}) %copy-start.5) | copy-done | bytes 536
  6.1 56.6 %lora_kv.1 = bf16[256,128]{1,0:T(8,128)(2,1)S(1)} custom-call(s32[1,256]{1,0:T(1,128)S(1)} %bitcast.2, s32[1,128]{1,0:T(1,128)S(1)} %bitcast.3, bf16[256,512]{1,0:T(8,128)(2,1)S(1)} %copy-done.3, bf16[512,2048]{1,0:T(8,128)(2,1)S(1)} %copy-done, bf16[4,512,128]{2,1,0:T(8,128)(2,1)S(1)} %copy-done.2, bf16[4,64,2048]{2,1,0:T(8,128)(2,1)S(1)} %copy-done.1), custom_call_target="tpu_custom_call" | custom-call | tf_op jit(solution)/shard_map/lora_kv/pallas_call | solution.py:315
  62.8 0.6 copy.8
Async XLA Ops:
  0.0 1.6 %copy-start = (bf16[512,2048]{1,0:T(8,128)(2,1)S(1)}, bf16[512,2048]{1,0:T(8,128)(2,1)}, u32[]{:S(2)}) copy-start(bf16[512,2048]{1,0:T(8,128)(2,1)} %kv_hbm.1) | copy-start | bytes 6291460
  1.6 1.2 %copy-start.1 = (bf16[4,64,2048]{2,1,0:T(8,128)(2,1)S(1)}, bf16[4,64,2048]{2,1,0:T(8,128)(2,1)}, u32[]{:S(2)}) copy-start(bf16[4,64,2048]{2,1,0:T(8,128)(2,1)} %up_hbm.1) | copy-start | bytes 3145732
  2.8 1.0 %copy-start.2 = (bf16[4,512,128]{2,1,0:T(8,128)(2,1)S(1)}, bf16[4,512,128]{2,1,0:T(8,128)(2,1)}, u32[]{:S(2)}) copy-start(bf16[4,512,128]{2,1,0:T(8,128)(2,1)} %down_hbm.1) | copy-start | bytes 1572868
  3.9 0.9 %copy-start.3 = (bf16[256,512]{1,0:T(8,128)(2,1)S(1)}, bf16[256,512]{1,0:T(8,128)(2,1)}, u32[]{:S(2)}) copy-start(bf16[256,512]{1,0:T(8,128)(2,1)} %tokens_hbm.1) | copy-start | bytes 786436
  4.8 0.7 %copy-start.4 = (s32[256,1]{0,1:T(1,128)S(1)}, s32[256,1]{0,1:T(1,128)}, u32[]{:S(2)}) copy-start(s32[256,1]{0,1:T(1,128)} %param.7) | copy-start | bytes 3076
  5.5 0.7 %copy-start.5 = (s32[128]{0:T(128)S(1)}, s32[128]{0:T(128)}, u32[]{:S(2)}) copy-start(s32[128]{0:T(128)} %param.8) | copy-start | bytes 1540

commit v2 on v1

v2 whole, which is shorter than its diff:
```python
import jax
import jax.numpy as jnp
from jax import lax
from jax.experimental import pallas as pl
from jax.experimental.pallas import tpu as pltpu
from jax.sharding import PartitionSpec as P

CENTRES = (6, -6, 3, -3, 0)
LEAVES = ((0, 2), (0, 1), (0, -1), (1, 1), (1, -1), (2, 1), (2, -1), (3, 1), (3, -1), (4, 1), (4, -1))
WINDOWS = ((0, 1), (2,), (3,), (4,))

adapter_scale = 0.5
MESH = pl.DeviceIdType.MESH
F32, BF16, I32 = jnp.float32, jnp.bfloat16, jnp.int32

NY, NX, NC, NZ = 4, 4, 2, 16
NA = NY * NX * NC
TOK, FEAT, COLS = 256, 512, 128
HELD, CAP, RANK2 = 4, 8, 128
MSG = HELD * CAP
GROUP = NX * NC
ROWS = GROUP * MSG
GROUPS = (2, 1, 3, 0)
OFFSETS = ((2, 0), (2, 1), (1, 0), (1, 1), (3, 0), (3, 1), (0, 1), (0, 0))


def iota(shape, dim):
    return lax.broadcasted_iota(I32, shape, dim)


def dot(a, b):
    return jnp.dot(a, b, preferred_element_type=F32)


def kernel(
    ids_hbm, table_hbm, tokens_hbm, kv_hbm, down_hbm, up_hbm, out_ref,
    ids, names_row, tok, kv, down, up, sbuf, rbuf, lbuf, ret, place, zsend, zrecv, pack,
    b1, own, r1, w2, r2,
    load_sem, self_sem, tok_send, tok_recv, ret_send, ret_recv, zs_send, zs_recv, zg_send, zg_recv,
    l1_send, l1_recv, l2_send, l2_recv, up_send, up_recv, far_sem, farther_sem,
):
    a, z = lax.axis_index("adapter"), lax.axis_index("tensor")
    y, x, c = lax.div(a, GROUP), lax.rem(lax.div(a, NC), NX), lax.rem(a, NC)
    pend = {}

    def at(dy, dx, dc):
        return (
            lax.rem(y + dy + NY, NY) * GROUP + lax.rem(x + dx + NX, NX) * NC + lax.rem(c + dc + NC, NC)
        )

    def along_z(dz):
        return lax.rem(z + dz + NZ, NZ)

    def plane_copy(src, dst, send, recv, peer):
        return pltpu.make_async_remote_copy(
            src, dst, send, recv, device_id={"adapter": peer}, device_id_type=MESH
        )

    def z_copy(src, dst, send, recv, peer):
        return pltpu.make_async_remote_copy(
            src, dst, send, recv, device_id={"tensor": peer}, device_id_type=MESH
        )

    def wait_bytes(ref, sem):
        pltpu.make_async_copy(ref, ref, sem).wait()

    def later(name, ref, sem):
        pend[name] = (ref, sem)

    def due(name):
        wait_bytes(*pend.pop(name))

    def signal_z(sem, dz):
        pl.semaphore_signal(sem, 1, device_id={"tensor": along_z(dz)}, device_id_type=MESH)

    loads = [
        pltpu.make_async_copy(ids_hbm, ids, load_sem.at[4]),
        pltpu.make_async_copy(table_hbm, names_row, load_sem.at[5]),
        pltpu.make_async_copy(tokens_hbm, tok, load_sem.at[0]),
        pltpu.make_async_copy(kv_hbm, kv, load_sem.at[1]),
        pltpu.make_async_copy(down_hbm, down, load_sem.at[2]),
        pltpu.make_async_copy(
            up_hbm.at[:, :, pl.ds(pl.multiple_of(z * COLS, COLS), COLS)], up.at[y, x, c], load_sem.at[3]
        ),
    ]
    for load in loads:
        load.start()

    barrier = pltpu.get_barrier_semaphore()

    @pl.loop(1, NA)
    def _(k):
        pl.semaphore_signal(barrier, 1, device_id={"adapter": lax.rem(a + k, NA)}, device_id_type=MESH)

    for dz in (1, -1, 2, -2):
        signal_z(barrier, dz)

    names = iota((128, TOK), 0)
    loads[0].wait()
    loads[1].wait()
    table = jnp.broadcast_to(names_row[...].astype(F32), (8, 128)).astype(BF16)
    hit_id = (names == ids[...]).astype(F32).astype(BF16)
    row = dot(table, hit_id)[0:1]
    hit = names == row.astype(I32)
    hit_f = hit.astype(F32)
    square0, square1 = iota((TOK, TOK), 0), iota((TOK, TOK), 1)
    earlier = dot(hit_f.astype(BF16), (square0 < square1).astype(F32).astype(BF16))
    within = jnp.sum(hit_f * earlier, axis=0, keepdims=True)
    slot = row.astype(I32) * CAP + within.astype(I32)

    def slots_of(r):
        return (((x + (r >> 6)) & (NX - 1)) << 6) | (((c + (r >> 5)) & (NC - 1)) << 5) | (r & (MSG - 1))

    def part(dz):
        d = along_z(dz)
        return dot(tok[...], kv[:, pl.ds(pl.multiple_of(d * COLS, COLS), COLS)])

    loads[2].wait()
    in_row = slots_of(square0)
    half = TOK // 2
    for turn, dy in enumerate(GROUPS):
        first = lax.rem(y + dy, NY) * ROWS
        chosen = (in_row == slot - first).astype(F32).astype(BF16)
        sbuf[dy * GROUP : (dy + 1) * GROUP] = dot(chosen, tok[...]).astype(BF16).reshape(GROUP, MSG, FEAT)
        if turn == 0:
            pl.semaphore_wait(barrier, NA - 1 + 4)
            signal_z(far_sem, 2)
            signal_z(far_sem, -2)
        for dx, dc in OFFSETS:
            k = dy * GROUP + dx * NC + dc
            if k == 0:
                copy = pltpu.make_async_copy(sbuf.at[0], rbuf.at[0], self_sem)
                later("self", sbuf.at[0], self_sem)
            else:
                copy = plane_copy(sbuf.at[k], rbuf.at[k], tok_send, tok_recv.at[dy], at(dy, dx, dc))
            copy.start()
        lo = dy * GROUP
        later(f"tok{dy}", rbuf.at[max(lo, 1) : lo + GROUP], tok_recv.at[dy])
        if turn == 0:
            loads[3].wait()
        for w in WINDOWS[turn]:
            for dz in (2, 1, -1) if w == 0 else (1, -1):
                k = LEAVES.index((w, dz))
                b1[k] = part(dz + CENTRES[w]).astype(BF16)
                z_copy(b1.at[k], r1.at[k], l1_send, l1_recv.at[w], along_z(dz)).start()
            k = LEAVES.index((w, 1))
            later(f"l1{w}", r1.at[0:3] if w == 0 else r1.at[k : k + 2], l1_recv.at[w])
    later("tok_send", sbuf.at[1:NA], tok_send)
    later("l1_send", b1, l1_send)
    for w in range(5):
        own[w] = part(CENTRES[w])
    pl.semaphore_wait(far_sem, 2)
    signal_z(farther_sem, 4)
    signal_z(farther_sem, -4)

    loads[5].wait()

    def first_axis(k):
        return jnp.where(c == 0, at(0, k, 0), at(k, 0, 0))

    for k in (2, 1, 3):
        plane_copy(up.at[y, x, c], up.at[y, x, c], up_send.at[0], up_recv.at[0], first_axis(k)).start()
    later("up0", up.at[0, 0:3, 0], up_recv.at[0])
    later("up_send0", up.at[0, 0:3, 0], up_send.at[0])

    diagonal = square0 == square1
    ones = jnp.ones((TOK, 128), BF16)
    row_at = dot(jnp.where(diagonal, row, 0.0).astype(BF16), ones)
    within_at = dot(jnp.where(diagonal, within, 0.0).astype(BF16), ones)
    slot_at = (row_at * CAP + within_at).astype(I32)
    slot_at = jnp.concatenate([slot_at, slot_at], axis=1)
    in_row = slots_of(square1)
    for dy in range(NY):
        first = lax.rem(y + dy, NY) * ROWS
        place[dy] = (in_row == slot_at - first).astype(F32).astype(BF16)

    loads[4].wait()
    left = jnp.concatenate([down[0], down[1]], axis=1)
    right = jnp.concatenate([down[2], down[3]], axis=1)
    which = (iota((ROWS, RANK2), 0) >> 3) & (HELD - 1)
    def window(w):
        due(f"l1{w}")
        k = LEAVES.index((w, 1))
        total = own[w] + r1[k].astype(F32) + r1[k + 1].astype(F32)
        return total + r1[0].astype(F32) if w == 0 else total

    def outer(w):
        w2[w] = window(w).astype(BF16)
        z_copy(w2.at[w], r2.at[w], l2_send, l2_recv.at[w], along_z(CENTRES[w] // 2)).start()
        later(f"l2{w}", r2.at[w], l2_recv.at[w])

    def inner(w):
        due(f"l2{w - 2}")
        w2[w] = (window(w) + r2[w - 2].astype(F32)).astype(BF16)
        z_copy(w2.at[w], r2.at[w], l2_send, l2_recv.at[w], along_z(CENTRES[w])).start()
        later(f"l2{w}", r2.at[w], l2_recv.at[w])

    def root():
        total = window(4)
        due("l22")
        due("l23")
        own[4] = total + r2[2].astype(F32) + r2[3].astype(F32)

    def token_step(dy):
        lo = dy * GROUP
        due(f"tok{dy}")
        if dy == 0:
            due("self")
        arrived = rbuf[lo : lo + GROUP].reshape(ROWS, FEAT)
        l01, l23 = dot(arrived, left), dot(arrived, right)
        low_rank = jnp.where(
            which < 2,
            jnp.where(which == 0, l01[:, :RANK2], l01[:, RANK2:]),
            jnp.where(which == 2, l23[:, :RANK2], l23[:, RANK2:]),
        ).astype(BF16)
        lbuf[lo : lo + GROUP] = low_rank.reshape(GROUP, MSG, RANK2)
        for dx, dc in OFFSETS:
            k = lo + dx * NC + dc
            if k == 0:
                ret[0] = lbuf[0]
            else:
                plane_copy(lbuf.at[k], ret.at[k], ret_send, ret_recv.at[dy], at(-dy, -dx, -dc)).start()
        later(f"ret{dy}", ret.at[max(lo, 1) : lo + GROUP], ret_recv.at[dy])
    outer(0)
    outer(1)
    token_step(2)
    token_step(1)
    inner(2)
    inner(3)
    token_step(3)
    token_step(0)
    later("l2_send", w2, l2_send)
    later("ret_send", lbuf.at[1:NA], ret_send)

    due("up0")

    @pl.when(c == 0)
    def _():
        for k in (2, 1, 3):
            plane_copy(up.at[y, :, 0], up.at[y, :, 0], up_send.at[1], up_recv.at[1], at(k, 0, 0)).start()

    @pl.when(c == 1)
    def _():
        for k in (2, 1, 3):
            plane_copy(up.at[:, x, 1], up.at[:, x, 1], up_send.at[1], up_recv.at[1], at(0, k, 0)).start()
    later("up1", up.at[0:3, :, 0], up_recv.at[1])
    later("up_send1", up.at[0:3, :, 0], up_send.at[1])

    low_rank = jnp.zeros((TOK, RANK2), F32)
    for dy in GROUPS:
        lo = dy * GROUP
        due(f"ret{dy}")
        low_rank += dot(place[dy], ret[lo : lo + GROUP].reshape(ROWS, RANK2))
    upper, lower = low_rank[:half], low_rank[half:]
    first_lanes = iota((half, RANK2), 1) < RANK2 // 2
    keys = jnp.where(first_lanes, upper, pltpu.roll(lower, RANK2 // 2, 1))
    values = jnp.where(first_lanes, pltpu.roll(upper, RANK2 // 2, 1), lower)
    zsend[0:8] = keys.astype(BF16).reshape(8, 16, RANK2)
    zsend[8:16] = values.astype(BF16).reshape(8, 16, RANK2)
    pl.semaphore_wait(farther_sem, 2)
    for k in (8, 7, 9, 6, 10, 5, 11, 4, 12, 3, 13, 2, 14, 1, 15):
        z_copy(zsend.at[along_z(k)], zrecv.at[k - 1], zs_send, zs_recv, along_z(k)).start()
    later("zs", zrecv, zs_recv)
    later("zs_send", zrecv, zs_send)

    due("zs")
    total = zsend[z].astype(F32)
    for k in range(NZ - 1):
        total += zrecv[k].astype(F32)
    spot, side = lax.rem(z, 8), lax.div(z, 8) * 8
    pack[spot] = total.astype(BF16)
    for k in (4, 3, 5, 2, 6, 1, 7):
        z_copy(pack.at[spot], pack.at[spot], zg_send, zg_recv, side + lax.rem(spot + k, 8)).start()
    later("zg", pack.at[0:7], zg_recv)
    later("zg_send", pack.at[0:7], zg_send)

    due("up1")
    other = at(0, 0, 1)
    plane_copy(up.at[:, :, c], up.at[:, :, c], up_send.at[2], up_recv.at[2], other).start()
    later("up2", up.at[:, :, 0], up_recv.at[2])
    later("up_send2", up.at[:, :, 0], up_send.at[2])

    root()

    due("zg")
    due("up2")

    full = pack[...].reshape(half, RANK2).astype(F32)
    turned = pltpu.roll(full, RANK2 // 2, 1)
    twice = jnp.concatenate(
        [jnp.where(first_lanes, full, turned), jnp.where(first_lanes, turned, full)], axis=0
    ).astype(BF16)
    twice = jnp.concatenate([twice, twice], axis=1)
    lane = iota((TOK, 256), 1) >> 6
    shifted = jnp.concatenate([row_at, row_at], axis=1).astype(I32) - lane
    delta = jnp.zeros((TOK, COLS), F32)
    for h in range(NA):
        block = jnp.where(shifted == HELD * h, twice, jnp.zeros_like(twice))
        delta += dot(block, up[h // GROUP, h // NC % NX, h % NC].reshape(HELD * 64, COLS))
    result = own[4] + adapter_scale * delta
    out_ref[...] = result.astype(BF16)
    for n in list(pend):
        due(n)


def per_device(tokens, token_adapter_index, adapter_table_row, kv_weight, down_weight, up_weight):
    dma = pltpu.SemaphoreType.DMA
    vmem = pltpu.VMEM
    call = pl.pallas_call(
        kernel,
        out_shape=jax.ShapeDtypeStruct((TOK, COLS), BF16),
        in_specs=[pl.BlockSpec(memory_space=pl.ANY)] * 6,
        out_specs=pl.BlockSpec(memory_space=pltpu.VMEM),
        scratch_shapes=[
            vmem((1, TOK), I32),
            vmem((1, 128), I32),
            vmem((TOK, FEAT), BF16),
            vmem((FEAT, NZ * COLS), BF16),
            vmem((HELD, FEAT, RANK2), BF16),
            vmem((NY, NX, NC, HELD, RANK2 // 2, COLS), BF16),
            vmem((NA, MSG, FEAT), BF16),
            vmem((NA, MSG, FEAT), BF16),
            vmem((NA, MSG, RANK2), BF16),
            vmem((NA, MSG, RANK2), BF16),
            vmem((NY, TOK, ROWS), BF16),
            vmem((NZ, 16, RANK2), BF16),
            vmem((NZ - 1, 16, RANK2), BF16),
            vmem((8, 16, RANK2), BF16),
            vmem((len(LEAVES), TOK, COLS), BF16),
            vmem((5, TOK, COLS), F32),
            vmem((len(LEAVES), TOK, COLS), BF16),
            vmem((4, TOK, COLS), BF16),
            vmem((4, TOK, COLS), BF16),
            dma((6,)),
            dma,
            dma,
            dma((NY,)),
            dma,
            dma((NY,)),
            dma,
            dma,
            dma,
            dma,
            dma,
            dma((5,)),
            dma,
            dma((4,)),
            dma((3,)),
            dma((3,)),
            pltpu.SemaphoreType.REGULAR,
            pltpu.SemaphoreType.REGULAR,
        ],
        compiler_params=pltpu.CompilerParams(
            collective_id=0, has_side_effects=True, vmem_limit_bytes=60 << 20
        ),
        name="lora_kv",
    )
    return call(
        token_adapter_index.reshape(1, TOK),
        adapter_table_row.reshape(1, 128),
        tokens,
        kv_weight,
        down_weight,
        up_weight,
    )


def solution(mesh):
    return jax.shard_map(
        per_device,
        mesh=mesh,
        in_specs=(
            P("adapter", "tensor"),
            P("adapter", None),
            P(),
            P("tensor", None),
            P("adapter", "tensor", None),
            P("adapter", None, None),
        ),
        out_specs=P("adapter", "tensor"),
        check_vma=False,
    )
```

time: 64 us -> 56.1 us (0.88)
  local copies, waits for them, and re-layouts: 6.77 us -> 1.47 us
  Pallas kernels: 56.6 us -> 54.4 us
    unnamed x13 -> x1, local copies, waits for them, and re-layouts: 6.77 us -> 1.47 us
    pallas_call x1, Pallas kernels: 56.6 us -> 54.4 us  [per_device(): call(token_adapter_index.reshape(1, TOK), adapter_table_row.reshape(1, 12...]
where the time goes in v2:
time: 56.1 us; the launch traced here: 55.9 us
  Pallas kernels  54.4 us (97%)
  local copies, waits for them, and re-layouts  1.47 us (3%)
    pallas_call x1, Pallas kernels, per_device(): call(token_adapter_index.reshape(1, TOK), adapter_table_row.reshape(1, 12...  54.4 us
    unnamed x1, local copies, waits for them, and re-layouts  1.47 us

profile of v2, /device:TPU:1, one launch (start us, length us, event | category | flops | bytes accessed | tf_op | source)
XLA Modules:
  0.0 55.9 jit_solution(14337742383224931931)
XLA Ops:
  0.0 54.4 %lora_kv.1 = bf16[256,128]{1,0:T(8,128)(2,1)} custom-call(s32[1,256]{1,0:T(1,128)} %bitcast.2, s32[1,128]{1,0:T(1,128)} %bitcast.3, bf16[256,512]{1,0:T(8,128)(2,1)} %tokens_hbm.1, bf16[512,2048]{1,0:T(8,128)(2,1)} %kv_hbm.1, bf16[4,512,128]{2,1,0:T(8,128)(2,1)} %down_hbm.1, bf16[4,64,2048]{2,1,0:T(8,128)(2,1)} %up_hbm.1), custom_call_target="tpu_custom_call" | custom-call | tf_op jit(solution)/shard_map/lora_kv/pallas_call | solution.py:358
  54.4 1.5 %copy.8 = bf16[256,128]{1,0:T(8,128)(2,1)} copy(bf16[256,128]{1,0:T(8,128)(2,1)} %lora_kv.1) | data formatting | bytes 131072

commit v3 on v2

--- a/solution.py
+++ b/solution.py
@@ -20,8 +20,10 @@
 MSG = HELD * CAP
 GROUP = NX * NC
 ROWS = GROUP * MSG
-GROUPS = (2, 1, 3, 0)
-OFFSETS = ((2, 0), (2, 1), (1, 0), (1, 1), (3, 0), (3, 1), (0, 1), (0, 0))
+GROUPS = (0, 1, 3, 2)
+MEMBERS = {
+    s: [(dy, (s - dy) % NX, dc, dy * NC + dc) for dy in (2, 1, 3, 0) for dc in (0, 1)] for s in GROUPS
+}
 
 
 def iota(shape, dim):
@@ -34,7 +36,7 @@
 
 def kernel(
     ids_hbm, table_hbm, tokens_hbm, kv_hbm, down_hbm, up_hbm, out_ref,
-    ids, names_row, tok, kv, down, up, sbuf, rbuf, lbuf, ret, place, zsend, zrecv, pack,
+    ids, names_row, tok, kv, down, up, sbuf, rbuf, lbuf, ret, place, zsend, zrecv, zown, pack,
     b1, own, r1, w2, r2,
     load_sem, self_sem, tok_send, tok_recv, ret_send, ret_recv, zs_send, zs_recv, zg_send, zg_recv,
     l1_send, l1_recv, l2_send, l2_recv, up_send, up_recv, far_sem, farther_sem,
@@ -108,31 +110,32 @@
     within = jnp.sum(hit_f * earlier, axis=0, keepdims=True)
     slot = row.astype(I32) * CAP + within.astype(I32)
 
-    def slots_of(r):
-        return (((x + (r >> 6)) & (NX - 1)) << 6) | (((c + (r >> 5)) & (NC - 1)) << 5) | (r & (MSG - 1))
+    def slots_of(r, s):
+        dy = r >> 6
+        row_first = ((y + dy) & (NY - 1)) << 8
+        chip_first = ((x + s + NX - dy) & (NX - 1)) << 6
+        return row_first | chip_first | (((c + (r >> 5)) & (NC - 1)) << 5) | (r & (MSG - 1))
 
     def part(dz):
         d = along_z(dz)
         return dot(tok[...], kv[:, pl.ds(pl.multiple_of(d * COLS, COLS), COLS)])
 
     loads[2].wait()
-    in_row = slots_of(square0)
     half = TOK // 2
     for turn, dy in enumerate(GROUPS):
-        first = lax.rem(y + dy, NY) * ROWS
-        chosen = (in_row == slot - first).astype(F32).astype(BF16)
+        chosen = (slots_of(square0, dy) == slot).astype(F32).astype(BF16)
         sbuf[dy * GROUP : (dy + 1) * GROUP] = dot(chosen, tok[...]).astype(BF16).reshape(GROUP, MSG, FEAT)
         if turn == 0:
             pl.semaphore_wait(barrier, NA - 1 + 4)
             signal_z(far_sem, 2)
             signal_z(far_sem, -2)
-        for dx, dc in OFFSETS:
-            k = dy * GROUP + dx * NC + dc
+        for my, mx, mc, i in MEMBERS[dy]:
+            k = dy * GROUP + i
             if k == 0:
                 copy = pltpu.make_async_copy(sbuf.at[0], rbuf.at[0], self_sem)
                 later("self", sbuf.at[0], self_sem)
             else:
-                copy = plane_copy(sbuf.at[k], rbuf.at[k], tok_send, tok_recv.at[dy], at(dy, dx, dc))
+                copy = plane_copy(sbuf.at[k], rbuf.at[k], tok_send, tok_recv.at[dy], at(my, mx, mc))
             copy.start()
         lo = dy * GROUP
         later(f"tok{dy}", rbuf.at[max(lo, 1) : lo + GROUP], tok_recv.at[dy])
@@ -158,21 +161,14 @@
     def first_axis(k):
         return jnp.where(c == 0, at(0, k, 0), at(k, 0, 0))
 
-    for k in (2, 1, 3):
-        plane_copy(up.at[y, x, c], up.at[y, x, c], up_send.at[0], up_recv.at[0], first_axis(k)).start()
-    later("up0", up.at[0, 0:3, 0], up_recv.at[0])
-    later("up_send0", up.at[0, 0:3, 0], up_send.at[0])
-
     diagonal = square0 == square1
     ones = jnp.ones((TOK, 128), BF16)
     row_at = dot(jnp.where(diagonal, row, 0.0).astype(BF16), ones)
     within_at = dot(jnp.where(diagonal, within, 0.0).astype(BF16), ones)
     slot_at = (row_at * CAP + within_at).astype(I32)
     slot_at = jnp.concatenate([slot_at, slot_at], axis=1)
-    in_row = slots_of(square1)
-    for dy in range(NY):
-        first = lax.rem(y + dy, NY) * ROWS
-        place[dy] = (in_row == slot_at - first).astype(F32).astype(BF16)
+    for dy in GROUPS:
+        place[dy] = (slots_of(square1, dy) == slot_at).astype(F32).astype(BF16)
 
     loads[4].wait()
     left = jnp.concatenate([down[0], down[1]], axis=1)
@@ -184,14 +180,24 @@
         total = own[w] + r1[k].astype(F32) + r1[k + 1].astype(F32)
         return total + r1[0].astype(F32) if w == 0 else total
 
+    def encode(w, total):
+        most = jnp.max(jnp.max(jnp.abs(total), axis=0, keepdims=True), axis=1, keepdims=True)
+        power = jnp.ceil(jnp.log2(jnp.maximum(most, 1e-30)) + 0.01)
+        w2[w, 0:TOK] = jnp.round(total * (32000.0 * jnp.exp2(-power))).astype(I32).astype(jnp.int16)
+        w2[w, TOK : TOK + 16] = jnp.broadcast_to(power, (16, COLS)).astype(I32).astype(jnp.int16)
+
+    def decode(w):
+        power = r2[w, TOK : TOK + 16].astype(I32).astype(F32)[0:1]
+        return r2[w, 0:TOK].astype(I32).astype(F32) * (jnp.exp2(power) * (1 / 32000.0))
+
     def outer(w):
-        w2[w] = window(w).astype(BF16)
+        encode(w, window(w))
         z_copy(w2.at[w], r2.at[w], l2_send, l2_recv.at[w], along_z(CENTRES[w] // 2)).start()
         later(f"l2{w}", r2.at[w], l2_recv.at[w])
 
     def inner(w):
         due(f"l2{w - 2}")
-        w2[w] = (window(w) + r2[w - 2].astype(F32)).astype(BF16)
+        encode(w, window(w) + decode(w - 2))
         z_copy(w2.at[w], r2.at[w], l2_send, l2_recv.at[w], along_z(CENTRES[w])).start()
         later(f"l2{w}", r2.at[w], l2_recv.at[w])
 
@@ -199,7 +205,7 @@
         total = window(4)
         due("l22")
         due("l23")
-        own[4] = total + r2[2].astype(F32) + r2[3].astype(F32)
+        own[4] = total + decode(2) + decode(3)
 
     def token_step(dy):
         lo = dy * GROUP
@@ -214,37 +220,28 @@
             jnp.where(which == 2, l23[:, :RANK2], l23[:, RANK2:]),
         ).astype(BF16)
         lbuf[lo : lo + GROUP] = low_rank.reshape(GROUP, MSG, RANK2)
-        for dx, dc in OFFSETS:
-            k = lo + dx * NC + dc
+        for my, mx, mc, i in MEMBERS[dy]:
+            k = lo + i
             if k == 0:
                 ret[0] = lbuf[0]
             else:
-                plane_copy(lbuf.at[k], ret.at[k], ret_send, ret_recv.at[dy], at(-dy, -dx, -dc)).start()
+                plane_copy(lbuf.at[k], ret.at[k], ret_send, ret_recv.at[dy], at(-my, -mx, -mc)).start()
         later(f"ret{dy}", ret.at[max(lo, 1) : lo + GROUP], ret_recv.at[dy])
+    token_step(GROUPS[0])
     outer(0)
     outer(1)
-    token_step(2)
-    token_step(1)
+    token_step(GROUPS[1])
+    token_step(GROUPS[2])
+    token_step(GROUPS[3])
     inner(2)
     inner(3)
-    token_step(3)
-    token_step(0)
     later("l2_send", w2, l2_send)
     later("ret_send", lbuf.at[1:NA], ret_send)
 
-    due("up0")
-
-    @pl.when(c == 0)
-    def _():
-        for k in (2, 1, 3):
-            plane_copy(up.at[y, :, 0], up.at[y, :, 0], up_send.at[1], up_recv.at[1], at(k, 0, 0)).start()
-
-    @pl.when(c == 1)
-    def _():
-        for k in (2, 1, 3):
-            plane_copy(up.at[:, x, 1], up.at[:, x, 1], up_send.at[1], up_recv.at[1], at(0, k, 0)).start()
-    later("up1", up.at[0:3, :, 0], up_recv.at[1])
-    later("up_send1", up.at[0:3, :, 0], up_send.at[1])
+    for k in (2, 1, 3):
+        plane_copy(up.at[y, x, c], up.at[y, x, c], up_send.at[0], up_recv.at[0], first_axis(k)).start()
+    later("up0", up.at[0, 0:3, 0], up_recv.at[0])
+    later("up_send0", up.at[0, 0:3, 0], up_send.at[0])
 
     low_rank = jnp.zeros((TOK, RANK2), F32)
     for dy in GROUPS:
@@ -259,20 +256,41 @@
     zsend[8:16] = values.astype(BF16).reshape(8, 16, RANK2)
     pl.semaphore_wait(farther_sem, 2)
     for k in (8, 7, 9, 6, 10, 5, 11, 4, 12, 3, 13, 2, 14, 1, 15):
-        z_copy(zsend.at[along_z(k)], zrecv.at[k - 1], zs_send, zs_recv, along_z(k)).start()
+        z_copy(zsend.at[along_z(k + 4 - NZ)], zrecv.at[k - 1], zs_send, zs_recv, along_z(k)).start()
     later("zs", zrecv, zs_recv)
     later("zs_send", zrecv, zs_send)
 
+    due("up0")
+
+    @pl.when(c == 0)
+    def _():
+        for k in (2, 1, 3):
+            plane_copy(up.at[y, :, 0], up.at[y, :, 0], up_send.at[1], up_recv.at[1], at(k, 0, 0)).start()
+
+    @pl.when(c == 1)
+    def _():
+        for k in (2, 1, 3):
+            plane_copy(up.at[:, x, 1], up.at[:, x, 1], up_send.at[1], up_recv.at[1], at(0, k, 0)).start()
+    later("up1", up.at[0:3, :, 0], up_recv.at[1])
+    later("up_send1", up.at[0:3, :, 0], up_send.at[1])
+
     due("zs")
-    total = zsend[z].astype(F32)
+    mine = along_z(4)
+    total = zsend[mine].astype(F32)
     for k in range(NZ - 1):
         total += zrecv[k].astype(F32)
-    spot, side = lax.rem(z, 8), lax.div(z, 8) * 8
-    pack[spot] = total.astype(BF16)
-    for k in (4, 3, 5, 2, 6, 1, 7):
-        z_copy(pack.at[spot], pack.at[spot], zg_send, zg_recv, side + lax.rem(spot + k, 8)).start()
-    later("zg", pack.at[0:7], zg_recv)
-    later("zg_send", pack.at[0:7], zg_send)
+    spot, side, spot_z = lax.rem(mine, 8), lax.div(mine, 8) * 8, lax.rem(z, 8)
+    zown[...] = total.astype(BF16)
+
+    @pl.when(spot >= 4)
+    def _():
+        pack[spot] = zown[...]
+
+    for t in (7, 6, 5, 4, 0, 1, 2, 3):
+
+        @pl.when(spot != t + 4)
+        def _(t=t):
+            z_copy(zown, pack.at[spot], zg_send, zg_recv, side + t).start()
 
     due("up1")
     other = at(0, 0, 1)
@@ -282,7 +300,14 @@
 
     root()
 
-    due("zg")
+    @pl.when(spot_z < 4)
+    def _():
+        wait_bytes(pack.at[0:7], zg_recv)
+
+    @pl.when(spot_z >= 4)
+    def _():
+        wait_bytes(pack, zg_recv)
+
     due("up2")
 
     full = pack[...].reshape(half, RANK2).astype(F32)
@@ -299,6 +324,15 @@
         delta += dot(block, up[h // GROUP, h // NC % NX, h % NC].reshape(HELD * 64, COLS))
     result = own[4] + adapter_scale * delta
     out_ref[...] = result.astype(BF16)
+
+    @pl.when(spot < 4)
+    def _():
+        wait_bytes(pack, zg_send)
+
+    @pl.when(spot >= 4)
+    def _():
+        wait_bytes(pack.at[0:7], zg_send)
+
     for n in list(pend):
         due(n)
 
@@ -325,12 +359,13 @@
             vmem((NY, TOK, ROWS), BF16),
             vmem((NZ, 16, RANK2), BF16),
             vmem((NZ - 1, 16, RANK2), BF16),
+            vmem((16, RANK2), BF16),
             vmem((8, 16, RANK2), BF16),
             vmem((len(LEAVES), TOK, COLS), BF16),
             vmem((5, TOK, COLS), F32),
             vmem((len(LEAVES), TOK, COLS), BF16),
-            vmem((4, TOK, COLS), BF16),
-            vmem((4, TOK, COLS), BF16),
+            vmem((4, TOK + 16, COLS), jnp.int16),
+            vmem((4, TOK + 16, COLS), jnp.int16),
             dma((6,)),
             dma,
             dma,

time: 56.1 us -> 52.6 us (0.938)
  Pallas kernels: 54.4 us -> 50.9 us
    pallas_call x1, Pallas kernels: 54.4 us -> 50.9 us  [per_device(): call(token_adapter_index.reshape(1, TOK), adapter_table_row.reshape(1, 12...]
where the time goes in v3:
time: 52.6 us; the launch traced here: 52.4 us
  Pallas kernels  50.9 us (97%)
  local copies, waits for them, and re-layouts  1.47 us (3%)
    pallas_call x1, Pallas kernels, per_device(): call(token_adapter_index.reshape(1, TOK), adapter_table_row.reshape(1, 12...  50.9 us
    unnamed x1, local copies, waits for them, and re-layouts  1.47 us

profile of v3, /device:TPU:1, one launch (start us, length us, event | category | flops | bytes accessed | tf_op | source)
XLA Modules:
  0.0 52.4 jit_solution(13584716805066420083)
XLA Ops:
  0.0 50.9 %lora_kv.1 = bf16[256,128]{1,0:T(8,128)(2,1)} custom-call(s32[1,256]{1,0:T(1,128)} %bitcast.2, s32[1,128]{1,0:T(1,128)} %bitcast.3, bf16[256,512]{1,0:T(8,128)(2,1)} %tokens_hbm.1, bf16[512,2048]{1,0:T(8,128)(2,1)} %kv_hbm.1, bf16[4,512,128]{2,1,0:T(8,128)(2,1)} %down_hbm.1, bf16[4,64,2048]{2,1,0:T(8,128)(2,1)} %up_hbm.1), custom_call_target="tpu_custom_call" | custom-call | tf_op jit(solution)/shard_map/lora_kv/pallas_call | solution.py:393
  50.9 1.5 %copy.8 = bf16[256,128]{1,0:T(8,128)(2,1)} copy(bf16[256,128]{1,0:T(8,128)(2,1)} %lora_kv.1) | data formatting | bytes 131072

commit v4 on v3

--- a/solution.py
+++ b/solution.py
@@ -20,10 +20,12 @@
 MSG = HELD * CAP
 GROUP = NX * NC
 ROWS = GROUP * MSG
-GROUPS = (0, 1, 3, 2)
-MEMBERS = {
-    s: [(dy, (s - dy) % NX, dc, dy * NC + dc) for dy in (2, 1, 3, 0) for dc in (0, 1)] for s in GROUPS
-}
+OFFSETS = sorted(
+    ((dy, dx, dc) for dy in range(NY) for dx in range(NX) for dc in range(NC)),
+    key=lambda o: (-min(o[0], NY - o[0]) - min(o[1], NX - o[1]), -o[2], o[0], o[1]),
+)
+GROUPS = [OFFSETS[i : i + GROUP] for i in range(0, NA, GROUP)]
+SELF = NA - 1
 
 
 def iota(shape, dim):
@@ -90,9 +92,8 @@
 
     barrier = pltpu.get_barrier_semaphore()
 
-    @pl.loop(1, NA)
-    def _(k):
-        pl.semaphore_signal(barrier, 1, device_id={"adapter": lax.rem(a + k, NA)}, device_id_type=MESH)
+    for offset in OFFSETS[:SELF]:
+        pl.semaphore_signal(barrier, 1, device_id={"adapter": at(*offset)}, device_id_type=MESH)
 
     for dz in (1, -1, 2, -2):
         signal_z(barrier, dz)
@@ -101,20 +102,18 @@
     loads[0].wait()
     loads[1].wait()
     table = jnp.broadcast_to(names_row[...].astype(F32), (8, 128)).astype(BF16)
-    hit_id = (names == ids[...]).astype(F32).astype(BF16)
-    row = dot(table, hit_id)[0:1]
-    hit = names == row.astype(I32)
-    hit_f = hit.astype(F32)
+    hit = (names == ids[...]).astype(F32)
     square0, square1 = iota((TOK, TOK), 0), iota((TOK, TOK), 1)
-    earlier = dot(hit_f.astype(BF16), (square0 < square1).astype(F32).astype(BF16))
-    within = jnp.sum(hit_f * earlier, axis=0, keepdims=True)
+    row = dot(table, hit.astype(BF16))[0:1]
+    earlier = dot(hit.astype(BF16), (square0 < square1).astype(F32).astype(BF16))
+    within = jnp.sum(hit * earlier, axis=0, keepdims=True)
     slot = row.astype(I32) * CAP + within.astype(I32)
 
-    def slots_of(r, s):
-        dy = r >> 6
-        row_first = ((y + dy) & (NY - 1)) << 8
-        chip_first = ((x + s + NX - dy) & (NX - 1)) << 6
-        return row_first | chip_first | (((c + (r >> 5)) & (NC - 1)) << 5) | (r & (MSG - 1))
+    def firsts(g):
+        return [at(*offset) * MSG for offset in GROUPS[g]]
+
+    def remote(g):
+        return slice(g * GROUP, min(g * GROUP + GROUP, SELF))
 
     def part(dz):
         d = along_z(dz)
@@ -122,25 +121,7 @@
 
     loads[2].wait()
     half = TOK // 2
-    for turn, dy in enumerate(GROUPS):
-        chosen = (slots_of(square0, dy) == slot).astype(F32).astype(BF16)
-        sbuf[dy * GROUP : (dy + 1) * GROUP] = dot(chosen, tok[...]).astype(BF16).reshape(GROUP, MSG, FEAT)
-        if turn == 0:
-            pl.semaphore_wait(barrier, NA - 1 + 4)
-            signal_z(far_sem, 2)
-            signal_z(far_sem, -2)
-        for my, mx, mc, i in MEMBERS[dy]:
-            k = dy * GROUP + i
-            if k == 0:
-                copy = pltpu.make_async_copy(sbuf.at[0], rbuf.at[0], self_sem)
-                later("self", sbuf.at[0], self_sem)
-            else:
-                copy = plane_copy(sbuf.at[k], rbuf.at[k], tok_send, tok_recv.at[dy], at(my, mx, mc))
-            copy.start()
-        lo = dy * GROUP
-        later(f"tok{dy}", rbuf.at[max(lo, 1) : lo + GROUP], tok_recv.at[dy])
-        if turn == 0:
-            loads[3].wait()
+    def leaves(turn):
         for w in WINDOWS[turn]:
             for dz in (2, 1, -1) if w == 0 else (1, -1):
                 k = LEAVES.index((w, dz))
@@ -148,7 +129,26 @@
                 z_copy(b1.at[k], r1.at[k], l1_send, l1_recv.at[w], along_z(dz)).start()
             k = LEAVES.index((w, 1))
             later(f"l1{w}", r1.at[0:3] if w == 0 else r1.at[k : k + 2], l1_recv.at[w])
-    later("tok_send", sbuf.at[1:NA], tok_send)
+    message = iota((MSG, TOK), 0)
+    for turn in range(len(GROUPS)):
+        chosen = jnp.concatenate([(message == slot - first).astype(F32) for first in firsts(turn)], axis=0)
+        sbuf[turn * GROUP : (turn + 1) * GROUP] = dot(chosen.astype(BF16), tok[...]).astype(BF16).reshape(GROUP, MSG, FEAT)
+        if turn == 0:
+            pl.semaphore_wait(barrier, NA - 1 + 4)
+            signal_z(far_sem, 2)
+            signal_z(far_sem, -2)
+        for i, offset in enumerate(GROUPS[turn]):
+            k = turn * GROUP + i
+            if k == SELF:
+                copy = pltpu.make_async_copy(sbuf.at[k], rbuf.at[k], self_sem)
+                later("self", sbuf.at[k], self_sem)
+            else:
+                copy = plane_copy(sbuf.at[k], rbuf.at[k], tok_send, tok_recv.at[turn], at(*offset))
+            copy.start()
+        later(f"tok{turn}", rbuf.at[remote(turn)], tok_recv.at[turn])
+    loads[3].wait()
+    for turn in range(4): leaves(turn)
+    later("tok_send", sbuf.at[0:SELF], tok_send)
     later("l1_send", b1, l1_send)
     for w in range(5):
         own[w] = part(CENTRES[w])
@@ -167,8 +167,12 @@
     within_at = dot(jnp.where(diagonal, within, 0.0).astype(BF16), ones)
     slot_at = (row_at * CAP + within_at).astype(I32)
     slot_at = jnp.concatenate([slot_at, slot_at], axis=1)
-    for dy in GROUPS:
-        place[dy] = (slots_of(square1, dy) == slot_at).astype(F32).astype(BF16)
+    lane = iota((8, ROWS), 1)
+    for g in range(len(GROUPS)):
+        slots = lane & (MSG - 1)
+        for i, first in enumerate(firsts(g)):
+            slots += jnp.where((lane >> 5) == i, first, 0)
+        place[g] = (slots[0:1] == slot_at).astype(F32).astype(BF16)
 
     loads[4].wait()
     left = jnp.concatenate([down[0], down[1]], axis=1)
@@ -207,10 +211,10 @@
         due("l23")
         own[4] = total + decode(2) + decode(3)
 
-    def token_step(dy):
-        lo = dy * GROUP
-        due(f"tok{dy}")
-        if dy == 0:
+    def token_step(g):
+        lo = g * GROUP
+        due(f"tok{g}")
+        if g == len(GROUPS) - 1:
             due("self")
         arrived = rbuf[lo : lo + GROUP].reshape(ROWS, FEAT)
         l01, l23 = dot(arrived, left), dot(arrived, right)
@@ -220,23 +224,22 @@
             jnp.where(which == 2, l23[:, :RANK2], l23[:, RANK2:]),
         ).astype(BF16)
         lbuf[lo : lo + GROUP] = low_rank.reshape(GROUP, MSG, RANK2)
-        for my, mx, mc, i in MEMBERS[dy]:
+        for i, (dy, dx, dc) in enumerate(GROUPS[g]):
             k = lo + i
-            if k == 0:
-                ret[0] = lbuf[0]
+            if k == SELF:
+                ret[k] = lbuf[k]
             else:
-                plane_copy(lbuf.at[k], ret.at[k], ret_send, ret_recv.at[dy], at(-my, -mx, -mc)).start()
-        later(f"ret{dy}", ret.at[max(lo, 1) : lo + GROUP], ret_recv.at[dy])
-    token_step(GROUPS[0])
+                plane_copy(lbuf.at[k], ret.at[k], ret_send, ret_recv.at[g], at(-dy, -dx, -dc)).start()
+        later(f"ret{g}", ret.at[remote(g)], ret_recv.at[g])
+
+    token_step(0)
     outer(0)
     outer(1)
-    token_step(GROUPS[1])
-    token_step(GROUPS[2])
-    token_step(GROUPS[3])
-    inner(2)
-    inner(3)
+    token_step(1)
+    token_step(2)
+    token_step(3)
     later("l2_send", w2, l2_send)
-    later("ret_send", lbuf.at[1:NA], ret_send)
+    later("ret_send", lbuf.at[0:SELF], ret_send)
 
     for k in (2, 1, 3):
         plane_copy(up.at[y, x, c], up.at[y, x, c], up_send.at[0], up_recv.at[0], first_axis(k)).start()
@@ -244,10 +247,9 @@
     later("up_send0", up.at[0, 0:3, 0], up_send.at[0])
 
     low_rank = jnp.zeros((TOK, RANK2), F32)
-    for dy in GROUPS:
-        lo = dy * GROUP
-        due(f"ret{dy}")
-        low_rank += dot(place[dy], ret[lo : lo + GROUP].reshape(ROWS, RANK2))
+    for g in range(len(GROUPS)):
+        due(f"ret{g}")
+        low_rank += dot(place[g], ret[g * GROUP : (g + 1) * GROUP].reshape(ROWS, RANK2))
     upper, lower = low_rank[:half], low_rank[half:]
     first_lanes = iota((half, RANK2), 1) < RANK2 // 2
     keys = jnp.where(first_lanes, upper, pltpu.roll(lower, RANK2 // 2, 1))
@@ -260,6 +262,8 @@
     later("zs", zrecv, zs_recv)
     later("zs_send", zrecv, zs_send)
 
+    inner(2)
+    inner(3)
     due("up0")
 
     @pl.when(c == 0)
@@ -286,7 +290,7 @@
     def _():
         pack[spot] = zown[...]
 
-    for t in (7, 6, 5, 4, 0, 1, 2, 3):
+    for t in (0, 1, 2, 3, 7, 6, 5, 4):
 
         @pl.when(spot != t + 4)
         def _(t=t):
@@ -316,8 +320,8 @@
         [jnp.where(first_lanes, full, turned), jnp.where(first_lanes, turned, full)], axis=0
     ).astype(BF16)
     twice = jnp.concatenate([twice, twice], axis=1)
-    lane = iota((TOK, 256), 1) >> 6
-    shifted = jnp.concatenate([row_at, row_at], axis=1).astype(I32) - lane
+    half_of = iota((TOK, 256), 1) >> 6
+    shifted = jnp.concatenate([row_at, row_at], axis=1).astype(I32) - half_of
     delta = jnp.zeros((TOK, COLS), F32)
     for h in range(NA):
         block = jnp.where(shifted == HELD * h, twice, jnp.zeros_like(twice))

time: 52.6 us -> 49.6 us (0.943)
  Pallas kernels: 50.9 us -> 47.4 us
    pallas_call x1, Pallas kernels: 50.9 us -> 47.4 us  [per_device(): call(token_adapter_index.reshape(1, TOK), adapter_table_row.reshape(1, 12...]
where the time goes in v4:
time: 49.6 us; the launch traced here: 48.9 us
  Pallas kernels  47.4 us (96%)
  local copies, waits for them, and re-layouts  1.47 us (3%)
    pallas_call x1, Pallas kernels, per_device(): call(token_adapter_index.reshape(1, TOK), adapter_table_row.reshape(1, 12...  47.4 us
    unnamed x1, local copies, waits for them, and re-layouts  1.47 us

profile of v4, /device:TPU:1, one launch (start us, length us, event | category | flops | bytes accessed | tf_op | source)
XLA Modules:
  0.0 48.9 jit_solution(5744380316599621243)
XLA Ops:
  0.0 47.4 %lora_kv.1 = bf16[256,128]{1,0:T(8,128)(2,1)} custom-call(s32[1,256]{1,0:T(1,128)} %bitcast.2, s32[1,128]{1,0:T(1,128)} %bitcast.3, bf16[256,512]{1,0:T(8,128)(2,1)} %tokens_hbm.1, bf16[512,2048]{1,0:T(8,128)(2,1)} %kv_hbm.1, bf16[4,512,128]{2,1,0:T(8,128)(2,1)} %down_hbm.1, bf16[4,64,2048]{2,1,0:T(8,128)(2,1)} %up_hbm.1), custom_call_target="tpu_custom_call" | custom-call | tf_op jit(solution)/shard_map/lora_kv/pallas_call | solution.py:397
  47.5 1.5 %copy.8 = bf16[256,128]{1,0:T(8,128)(2,1)} copy(bf16[256,128]{1,0:T(8,128)(2,1)} %lora_kv.1) | data formatting | bytes 131072

commit v5 on v4

--- a/solution.py
+++ b/solution.py
@@ -37,7 +37,7 @@
 
 
 def kernel(
-    ids_hbm, table_hbm, tokens_hbm, kv_hbm, down_hbm, up_hbm, out_ref,
+    ids_hbm, tokens_hbm, kv_hbm, down_hbm, up_hbm, out_ref,
     ids, names_row, tok, kv, down, up, sbuf, rbuf, lbuf, ret, place, zsend, zrecv, zown, pack,
     b1, own, r1, w2, r2,
     load_sem, self_sem, tok_send, tok_recv, ret_send, ret_recv, zs_send, zs_recv, zg_send, zg_recv,
@@ -78,8 +78,8 @@
         pl.semaphore_signal(sem, 1, device_id={"tensor": along_z(dz)}, device_id_type=MESH)
 
     loads = [
-        pltpu.make_async_copy(ids_hbm, ids, load_sem.at[4]),
-        pltpu.make_async_copy(table_hbm, names_row, load_sem.at[5]),
+        pltpu.make_async_copy(ids_hbm.at[:, :TOK], ids, load_sem.at[4]),
+        pltpu.make_async_copy(ids_hbm.at[:, TOK:], names_row, load_sem.at[5]),
         pltpu.make_async_copy(tokens_hbm, tok, load_sem.at[0]),
         pltpu.make_async_copy(kv_hbm, kv, load_sem.at[1]),
         pltpu.make_async_copy(down_hbm, down, load_sem.at[2]),
@@ -232,9 +232,9 @@
                 plane_copy(lbuf.at[k], ret.at[k], ret_send, ret_recv.at[g], at(-dy, -dx, -dc)).start()
         later(f"ret{g}", ret.at[remote(g)], ret_recv.at[g])
 
-    token_step(0)
     outer(0)
     outer(1)
+    token_step(0)
     token_step(1)
     token_step(2)
     token_step(3)
@@ -302,6 +302,10 @@
     later("up2", up.at[:, :, 0], up_recv.at[2])
     later("up_send2", up.at[:, :, 0], up_send.at[2])
 
+    half_of = iota((TOK, 256), 1) >> 6
+    shifted = jnp.concatenate([row_at, row_at], axis=1) - half_of.astype(F32)
+    shifted = shifted.astype(BF16)
+
     root()
 
     @pl.when(spot_z < 4)
@@ -320,11 +324,9 @@
         [jnp.where(first_lanes, full, turned), jnp.where(first_lanes, turned, full)], axis=0
     ).astype(BF16)
     twice = jnp.concatenate([twice, twice], axis=1)
-    half_of = iota((TOK, 256), 1) >> 6
-    shifted = jnp.concatenate([row_at, row_at], axis=1).astype(I32) - half_of
     delta = jnp.zeros((TOK, COLS), F32)
     for h in range(NA):
-        block = jnp.where(shifted == HELD * h, twice, jnp.zeros_like(twice))
+        block = jnp.where(shifted == jnp.asarray(HELD * h, shifted.dtype), twice, jnp.zeros_like(twice))
         delta += dot(block, up[h // GROUP, h // NC % NX, h % NC].reshape(HELD * 64, COLS))
     result = own[4] + adapter_scale * delta
     out_ref[...] = result.astype(BF16)
@@ -347,7 +349,7 @@
     call = pl.pallas_call(
         kernel,
         out_shape=jax.ShapeDtypeStruct((TOK, COLS), BF16),
-        in_specs=[pl.BlockSpec(memory_space=pl.ANY)] * 6,
+        in_specs=[pl.BlockSpec(memory_space=pl.ANY)] * 5,
         out_specs=pl.BlockSpec(memory_space=pltpu.VMEM),
         scratch_shapes=[
             vmem((1, TOK), I32),
@@ -390,13 +392,12 @@
             pltpu.SemaphoreType.REGULAR,
         ],
         compiler_params=pltpu.CompilerParams(
-            collective_id=0, has_side_effects=True, vmem_limit_bytes=60 << 20
+            collective_id=0, has_side_effects=True, vmem_limit_bytes=55100 << 10
         ),
         name="lora_kv",
     )
     return call(
-        token_adapter_index.reshape(1, TOK),
-        adapter_table_row.reshape(1, 128),
+        jnp.concatenate([token_adapter_index.reshape(1, TOK), adapter_table_row.reshape(1, 128)], axis=1),
         tokens,
         kv_weight,
         down_weight,

time: 49.6 us -> 48.3 us (0.974); the launches traced: 48.9 us -> 48.1 us
  local copies, waits for them, and re-layouts: 1.47 us -> 0.63 us
  other arithmetic: 0 us -> 0.7 us
  Pallas kernels: 47.4 us -> 46.8 us
    unnamed x1, local copies, waits for them, and re-layouts: 1.47 us -> 0.63 us
    concatenate x0 -> x1, other arithmetic: none -> 0.7 us  [per_device(): jnp.concatenate([token_adapter_index.reshape(1, TOK), adapter_table_row.r...]
    pallas_call x1, Pallas kernels: 47.4 us -> 46.8 us  [per_device(): call(jnp.concatenate([token_adapter_index.reshape(1, TOK), adapter_table_...]
where the time goes in v5:
time: 48.3 us; the launch traced here: 48.1 us
  Pallas kernels  46.8 us (97%)
  other arithmetic  0.7 us (1%)
  local copies, waits for them, and re-layouts  0.63 us (1%)
    pallas_call x1, Pallas kernels, per_device(): call(jnp.concatenate([token_adapter_index.reshape(1, TOK), adapter_table_...  46.8 us

profile of v5, /device:TPU:1, one launch (start us, length us, event | category | flops | bytes accessed | tf_op | source)
XLA Modules:
  0.0 48.1 jit_solution(8535309779585900788)
XLA Ops:
  0.0 0.7 %pad_add_fusion.ids_hbm = s32[1,384]{1,0:T(1,128)S(1)} fusion(s32[1,128]{1,0:T(1,128)} %bitcast.3, s32[1,256]{1,0:T(1,128)} %bitcast.2), kind=kLoop, calls=%fused_computation | loop fusion | flops 384 | bytes 3072 | tf_op jit(solution)/shard_map/concatenate | solution.py:400
  0.7 46.8 %lora_kv.1 = bf16[256,128]{1,0:T(8,128)(2,1)S(1)} custom-call(s32[1,384]{1,0:T(1,128)S(1)} %pad_add_fusion.ids_hbm, bf16[256,512]{1,0:T(8,128)(2,1)} %tokens_hbm.1, bf16[512,2048]{1,0:T(8,128)(2,1)} %kv_hbm.1, bf16[4,512,128]{2,1,0:T(8,128)(2,1)} %down_hbm.1, bf16[4,64,2048]{2,1,0:T(8,128)(2,1)} %up_hbm.1), custom_call_target="tpu_custom_call" | custom-call | tf_op jit(solution)/shard_map/lora_kv/pallas_call | solution.py:399
  47.5 0.6 %copy.8 = bf16[256,128]{1,0:T(8,128)(2,1)} copy(bf16[256,128]{1,0:T(8,128)(2,1)S(1)} %lora_kv.1) | data formatting | bytes 131072

commit v6 on v5

--- a/solution.py
+++ b/solution.py
@@ -37,8 +37,8 @@
 
 
 def kernel(
-    ids_hbm, tokens_hbm, kv_hbm, down_hbm, up_hbm, out_ref,
-    ids, names_row, tok, kv, down, up, sbuf, rbuf, lbuf, ret, place, zsend, zrecv, zown, pack,
+    ids_ref, tokens_hbm, kv_hbm, down_hbm, up_hbm, out_ref,
+    tok, kv, down, up, sbuf, rbuf, lbuf, ret, place, zsend, zrecv, zown, pack,
     b1, own, r1, w2, r2,
     load_sem, self_sem, tok_send, tok_recv, ret_send, ret_recv, zs_send, zs_recv, zg_send, zg_recv,
     l1_send, l1_recv, l2_send, l2_recv, up_send, up_recv, far_sem, farther_sem,
@@ -78,8 +78,6 @@
         pl.semaphore_signal(sem, 1, device_id={"tensor": along_z(dz)}, device_id_type=MESH)
 
     loads = [
-        pltpu.make_async_copy(ids_hbm.at[:, :TOK], ids, load_sem.at[4]),
-        pltpu.make_async_copy(ids_hbm.at[:, TOK:], names_row, load_sem.at[5]),
         pltpu.make_async_copy(tokens_hbm, tok, load_sem.at[0]),
         pltpu.make_async_copy(kv_hbm, kv, load_sem.at[1]),
         pltpu.make_async_copy(down_hbm, down, load_sem.at[2]),
@@ -99,10 +97,8 @@
         signal_z(barrier, dz)
 
     names = iota((128, TOK), 0)
-    loads[0].wait()
-    loads[1].wait()
-    table = jnp.broadcast_to(names_row[...].astype(F32), (8, 128)).astype(BF16)
-    hit = (names == ids[...]).astype(F32)
+    table = jnp.broadcast_to(ids_ref[:, TOK:].astype(F32), (8, 128)).astype(BF16)
+    hit = (names == ids_ref[:, :TOK]).astype(F32)
     square0, square1 = iota((TOK, TOK), 0), iota((TOK, TOK), 1)
     row = dot(table, hit.astype(BF16))[0:1]
     earlier = dot(hit.astype(BF16), (square0 < square1).astype(F32).astype(BF16))
@@ -119,7 +115,7 @@
         d = along_z(dz)
         return dot(tok[...], kv[:, pl.ds(pl.multiple_of(d * COLS, COLS), COLS)])
 
-    loads[2].wait()
+    loads[0].wait()
     half = TOK // 2
     def leaves(turn):
         for w in WINDOWS[turn]:
@@ -130,9 +126,15 @@
             k = LEAVES.index((w, 1))
             later(f"l1{w}", r1.at[0:3] if w == 0 else r1.at[k : k + 2], l1_recv.at[w])
     message = iota((MSG, TOK), 0)
-    for turn in range(len(GROUPS)):
+    def fill(turn):
         chosen = jnp.concatenate([(message == slot - first).astype(F32) for first in firsts(turn)], axis=0)
         sbuf[turn * GROUP : (turn + 1) * GROUP] = dot(chosen.astype(BF16), tok[...]).astype(BF16).reshape(GROUP, MSG, FEAT)
+
+    fill(0)
+    fill(1)
+    for turn in range(len(GROUPS)):
+        if turn > 1:
+            fill(turn)
         if turn == 0:
             pl.semaphore_wait(barrier, NA - 1 + 4)
             signal_z(far_sem, 2)
@@ -146,7 +148,7 @@
                 copy = plane_copy(sbuf.at[k], rbuf.at[k], tok_send, tok_recv.at[turn], at(*offset))
             copy.start()
         later(f"tok{turn}", rbuf.at[remote(turn)], tok_recv.at[turn])
-    loads[3].wait()
+    loads[1].wait()
     for turn in range(4): leaves(turn)
     later("tok_send", sbuf.at[0:SELF], tok_send)
     later("l1_send", b1, l1_send)
@@ -156,7 +158,7 @@
     signal_z(farther_sem, 4)
     signal_z(farther_sem, -4)
 
-    loads[5].wait()
+    loads[3].wait()
 
     def first_axis(k):
         return jnp.where(c == 0, at(0, k, 0), at(k, 0, 0))
@@ -174,7 +176,7 @@
             slots += jnp.where((lane >> 5) == i, first, 0)
         place[g] = (slots[0:1] == slot_at).astype(F32).astype(BF16)
 
-    loads[4].wait()
+    loads[2].wait()
     left = jnp.concatenate([down[0], down[1]], axis=1)
     right = jnp.concatenate([down[2], down[3]], axis=1)
     which = (iota((ROWS, RANK2), 0) >> 3) & (HELD - 1)
@@ -349,11 +351,9 @@
     call = pl.pallas_call(
         kernel,
         out_shape=jax.ShapeDtypeStruct((TOK, COLS), BF16),
-        in_specs=[pl.BlockSpec(memory_space=pl.ANY)] * 5,
+        in_specs=[pl.BlockSpec(memory_space=pltpu.VMEM)] + [pl.BlockSpec(memory_space=pl.ANY)] * 4,
         out_specs=pl.BlockSpec(memory_space=pltpu.VMEM),
         scratch_shapes=[
-            vmem((1, TOK), I32),
-            vmem((1, 128), I32),
             vmem((TOK, FEAT), BF16),
             vmem((FEAT, NZ * COLS), BF16),
             vmem((HELD, FEAT, RANK2), BF16),
@@ -372,7 +372,7 @@
             vmem((len(LEAVES), TOK, COLS), BF16),
             vmem((4, TOK + 16, COLS), jnp.int16),
             vmem((4, TOK + 16, COLS), jnp.int16),
-            dma((6,)),
+            dma((4,)),
             dma,
             dma,
             dma((NY,)),

time: 48.3 us -> 48.2 us (level)
  no operation moved by 1% of the time
where the time goes in v6:
time: 48.2 us; the launch traced here: 47.8 us
  Pallas kernels  46.4 us (96%)
  other arithmetic  0.7 us (1%)
  local copies, waits for them, and re-layouts  0.63 us (1%)
    pallas_call x1, Pallas kernels, per_device(): call(jnp.concatenate([token_adapter_index.reshape(1, TOK), adapter_table_...  46.4 us

profile of v6, /device:TPU:1, one launch (start us, length us, event | category | flops | bytes accessed | tf_op | source)
XLA Modules:
  0.0 47.8 jit_solution(8973968248210225421)
XLA Ops:
  0.0 0.7 %pad_add_fusion.ids_ref = s32[1,384]{1,0:T(1,128)S(1)} fusion(s32[1,128]{1,0:T(1,128)} %bitcast.3, s32[1,256]{1,0:T(1,128)} %bitcast.2), kind=kLoop, calls=%fused_computation | loop fusion | flops 384 | bytes 3072 | tf_op jit(solution)/shard_map/concatenate | solution.py:400
  0.7 46.4 %lora_kv.1 = bf16[256,128]{1,0:T(8,128)(2,1)S(1)} custom-call(s32[1,384]{1,0:T(1,128)S(1)} %pad_add_fusion.ids_ref, bf16[256,512]{1,0:T(8,128)(2,1)} %tokens_hbm.1, bf16[512,2048]{1,0:T(8,128)(2,1)} %kv_hbm.1, bf16[4,512,128]{2,1,0:T(8,128)(2,1)} %down_hbm.1, bf16[4,64,2048]{2,1,0:T(8,128)(2,1)} %up_hbm.1), custom_call_target="tpu_custom_call" | custom-call | tf_op jit(solution)/shard_map/lora_kv/pallas_call | solution.py:399
  47.1 0.6 %copy.8 = bf16[256,128]{1,0:T(8,128)(2,1)} copy(bf16[256,128]{1,0:T(8,128)(2,1)S(1)} %lora_kv.1) | data formatting | bytes 131072
